TPU v7x, 32 devices: a whole 2x2x4 slice. The times are simulated.
32 devices in a mesh: row: 4 (over y, x), col: 4 (over z), depth: 2 (over core).
Axes of the slice: x: 2, y: 2, z: 4, core: 2. Of those that a mesh axis runs over, the one named last changes fastest.
Arguments:
- matrix: float32 [6144, 6144], P('row', ('col', 'depth')), as said below
- occupancy: int32 [48, 48], replicated, may hold values from 0 to 1, as said below
- pattern: int32 [48, 48], replicated, may hold values 0 or 1
Outputs:
- square: float32 [6144, 6144], P('row', ('col', 'depth'))
Inputs may be any that keep to these rules, and one draw needn't show every extreme that they name: matrix is symmetric. occupancy is symmetric, every diagonal block is occupied, and every block row holds exactly 4 occupied blocks.
All inputs are finite; a program needn't handle non-finite values.
Results may differ from a plain program's by a relative error of at most 0.000055.
Values sent between devices are 32-bit elements; how exact they have to be, the bound alone decides.
No kernel may reach another device: no remote copies, remote signals or barrier semaphores. Data moves between devices by JAX's collectives and lax.ppermute only.
A program may use at most 192 MiB of HBM per device.

v0:
```python
import jax
import jax.numpy as jnp
from jax import lax
from jax.sharding import PartitionSpec as P

BS = 128


def expand_mask(mask):
    return jnp.repeat(jnp.repeat(mask.astype(jnp.float32), BS, axis=0), BS, axis=1)


def shards(matrix, occupancy, pattern):
    rows = matrix.shape[0]
    cols = matrix.shape[1]
    row_blocks = rows // BS
    col_blocks = cols // BS
    row_place = lax.axis_index("row") * row_blocks
    col_place = lax.axis_index(("col", "depth")) * col_blocks
    own_occ = lax.dynamic_slice(occupancy, (row_place, col_place), (row_blocks, col_blocks))
    own_pattern = lax.dynamic_slice(pattern, (row_place, col_place), (row_blocks, col_blocks))
    masked = matrix * expand_mask(own_occ)
    left_panel = lax.all_gather(masked, ("col", "depth"), axis=1, tiled=True)
    product = jnp.dot(
        left_panel,
        lax.all_gather(masked, "row", axis=0, tiled=True),
        precision=lax.Precision.HIGHEST,
        preferred_element_type=jnp.float32,
    )
    return product * expand_mask(own_pattern)


def solution(mesh):
    return jax.shard_map(
        shards,
        mesh=mesh,
        in_specs=(P("row", ("col", "depth")), P(), P()),
        out_specs=P("row", ("col", "depth")),
        check_vma=False,
    )
```

profile of v0, /device:TPU:11, one launch (start us, length us, event | category | flops | bytes accessed | tf_op | source)
XLA Modules:
  0.0 710.2 jit_solution(9948927619952013068)
XLA Ops:
  6.5 0.0 all-gather.5.cloned.1.call-start
  6.5 0.8 dynamic_slice.6
  7.3 0.1 copy.12
  7.4 0.1 broadcast_bitcast_fusion.1
  7.5 6.0 copy.9
  13.6 5.0 bitcast_multiply_fusion
  18.5 0.0 all-gather.5.cloned.1.call-update
  18.6 0.0 all-gather.3.cloned.1.call-start
  18.6 0.7 all-gather.3.cloned.1.call-update
  19.3 0.8 dynamic_slice.7
  20.1 0.1 copy.13
  20.2 0.1 broadcast_bitcast_fusion
  20.3 2.8 broadcast_in_dim.15
  23.1 6.1 copy.11
  29.2 166.6 %all-gather.5.cloned.1.call-done = f32[6144,768]{0,1:T(8,128)} async-done(((f32[1536,768]{0,1:T(8,128)}), f32[6144,768]{0,1:T(8,128)}) %all-gather.5.cloned.1.call-update) | async-done | bytes 18874384 | tf_op jit(solution)/shard_map/all_gather | solution.py:26
  195.8 324.5 %all-gather.3.cloned.1.call-done = f32[1536,6144]{0,1:T(8,128)} async-done(((f32[1536,768]{0,1:T(8,128)}), f32[1536,6144]{0,1:T(8,128)}) %all-gather.3.cloned.1.call-update) | async-done | bytes 37748752 | tf_op jit(solution)/shard_map/all_gather | solution.py:23
  520.3 183.1 %convolution_multiply_fusion = f32[1536,768]{1,0:T(8,128)} fusion(f32[1536,768]{1,0:T(8,128)} %copy.11, f32[1536,6144]{0,1:T(8,128)} %all-gather.3.cloned.1.call-done, f32[6144,768]{0,1:T(8,128)} %all-gather.5.cloned.1.call-done), kind=kOutput, calls=%fused_computation.1 | convolution fusion | flops 86974267392 | bytes 66060288 | tf_op jit(solution)/shard_map/dot_general | solution.py:24
  (4 shorter events, 0.0 us)
Async XLA Ops:
  6.5 189.3 %all-gather.5.cloned.1.call-start = ((), (), s32[]{:S(2)}) async-start(), calls=%async_computation.1 | async-start | bytes 23592960 | tf_op jit(solution)/shard_map/all_gather | solution.py:26
  18.6 501.8 %all-gather.3.cloned.1.call-start = ((), (), s32[]{:S(2)}) async-start(), calls=%async_computation | async-start | bytes 42467328 | tf_op jit(solution)/shard_map/all_gather | solution.py:23
Sparse Core Ops, SparseCore 0:
  18.7 177.0 all-gather.4
  197.4 322.8 all-gather.2
where the time goes:
time: 714 us; the launch traced here: 710 us
  waiting for transfers between devices  492 us (69%)
  matrix products  183 us (26%)
  local copies, waits for them, and re-layouts  16.9 us (2%)
  between operations  13.4 us (2%)
    all_gather x1, waiting for transfers between devices, shards(): left_panel = lax.all_gather(masked, ('col', 'depth'), axis=1, tiled=True)  325 us
    dot_general x1, matrix products, shards(): jnp.dot(left_panel, lax.all_gather(masked, 'row', axis=0, tiled=True), pr...  183 us
    all_gather x1, waiting for transfers between devices, shards(): lax.all_gather(masked, 'row', axis=0, tiled=True)  167 us
  transfers between devices with their start and end apart: 2, of which 2 were waited for; matrix products, arithmetic and copies ran while one was open for 1% of the time, Pallas kernels for 0%

commit v1 on v0

v1 whole, which is shorter than its diff:
```python
import functools

import jax
import jax.numpy as jnp
from jax import lax
from jax.experimental import pallas as pl
from jax.experimental.pallas import tpu as pltpu
from jax.sharding import PartitionSpec as P

BS = 128
KB = 4
NONE = 31
GROUP = 4
PAT_BIT = 20
PLAIN, LOWER, UPPER = 0, 1, 2


class Sizes:
    def __init__(self, mesh, matrix_shape):
        self.n_row = mesh.shape["row"]
        self.n_col = mesh.shape["col"]
        self.n_depth = mesh.shape["depth"]
        self.nb = matrix_shape[0] // BS
        self.rows = self.nb // self.n_row
        self.cols = self.nb // (self.n_col * self.n_depth)
        self.pairs = (min(self.rows, self.cols) + 1) // 2
        self.own = KB * self.cols
        self.n_a = KB * self.rows
        self.n_out = self.rows * self.cols
        self.cap = KB * min(self.rows, self.cols)
        self.x_tables = -(-self.n_row // GROUP)
        self.z_tables = -(-self.n_col // GROUP)
        self.tables = self.x_tables + self.z_tables
        self.buckets = []
        for far, near in ((5, 12), (6, 12), (7, 12), (8, 14), (9, 14), (11, 16)):
            if near < self.cap:
                self.buckets.append((far, near))
        self.buckets.append((self.cap, self.cap))


def group_of(place, size, count):
    group = jnp.zeros_like(place)
    for g in range(1, count):
        group = group + (place >= g * size).astype(jnp.int32)
    return group


def ones_dot(a, b):
    return jnp.dot(a.astype(jnp.bfloat16), b.astype(jnp.bfloat16), preferred_element_type=jnp.float32)


def table_kernel(sz, occ_ref, pat_ref, table_ref, near_ref, bucket_ref):
    nb = sz.nb
    occ = (occ_ref[...] != 0).astype(jnp.float32)
    pat = (pat_ref[...] != 0).astype(jnp.float32)
    row_i = lax.broadcasted_iota(jnp.int32, (nb, nb), 0)
    col_i = lax.broadcasted_iota(jnp.int32, (nb, nb), 1)
    off = jnp.where(row_i == col_i, 0.0, occ)
    row_rg = group_of(row_i, sz.rows, sz.n_row)
    col_rg = group_of(col_i, sz.rows, sz.n_row)
    row_cg = group_of(row_i, sz.cols, sz.n_col * sz.n_depth)
    col_cg = group_of(col_i, sz.cols, sz.n_col * sz.n_depth)
    col_zg = group_of(col_i, sz.cols * sz.n_depth, sz.n_col)
    same = row_cg == col_cg
    before = (same & (row_i < col_i)).astype(jnp.float32)
    same = same.astype(jnp.float32)
    above = ((row_rg == col_rg) & (col_i < row_i)).astype(jnp.float32)
    first = jnp.maximum(row_rg * sz.rows, col_cg * sz.cols)
    last = jnp.minimum((row_rg + 1) * sz.rows, (col_cg + 1) * sz.cols)
    skip = jnp.where(first < last, sz.pairs, 0)

    def codes(need, sent):
        listed = jnp.where(need > 0, off, 0.0)
        rank = ones_dot(listed, before) + ones_dot(above, ones_dot(listed, same))
        rank = rank.astype(jnp.int32) + skip
        used = jnp.where(listed > 0, rank + 1, skip)
        return jnp.where(listed > 0, jnp.minimum(rank, NONE - 1), NONE), jnp.where(sent, used, 0), jnp.where(sent, 0, used)

    far = jnp.zeros((nb, nb), jnp.int32)
    near = jnp.zeros((nb, nb), jnp.int32)
    tables = [jnp.zeros((nb, nb), jnp.int32) for _ in range(sz.tables)]
    for r in range(sz.n_row):
        need = ones_dot(jnp.where(col_rg == r, occ, 0.0), pat)
        code, count, _ = codes(need, row_rg != r)
        far = jnp.maximum(far, count)
        tables[r // GROUP] += code << (5 * (r % GROUP))
    for z in range(sz.n_col):
        need = ones_dot(jnp.where(col_zg == z, pat, 0.0), occ)
        code, count, here = codes(need, col_zg != z)
        far = jnp.maximum(far, count)
        near = jnp.maximum(near, here)
        tables[sz.x_tables + z // GROUP] += code << (5 * (z % GROUP))
    tables[0] += pat.astype(jnp.int32) << PAT_BIT
    for t in range(sz.tables):
        table_ref[t] = tables[t]

    lower = (col_i < row_i).astype(jnp.float32)
    order = ones_dot(lower, occ).astype(jnp.int32)
    weight = jnp.where(occ > 0, row_i << (6 * jnp.minimum(order, KB - 1)), 0)
    near_ref[...] = jnp.sum(weight, axis=0, keepdims=True)
    far_max = jnp.max(far)
    near_max = jnp.max(near)
    bucket = jnp.int32(0)
    for c, s in sz.buckets[:-1]:
        bucket = bucket + jnp.where((far_max <= c) & (near_max <= s), 0, 1)
    bucket_ref[0] = bucket


def neighbour(near_ref, block, s):
    return (near_ref[0, block] >> (6 * s)) & 63


def slot_of(near_ref, block, other):
    slot = jnp.int32(0)
    for u in range(KB):
        slot = slot + (neighbour(near_ref, block, u) < other).astype(jnp.int32)
    return slot


def code_at(table_ref, i, k, group, base):
    word = table_ref[base + group // GROUP, i, k]
    return (word >> (5 * (group % GROUP))) & 31


def place(ref, slot):
    return ref.at[pl.ds(pl.multiple_of(slot * BS, BS), BS), :]


def block_at(ref, i, j):
    return ref.at[pl.ds(pl.multiple_of(i * BS, BS), BS), pl.ds(pl.multiple_of(j * BS, BS), BS)]


def pack_kernel(sz, table_ref, near_ref, matrix_ref, own_ref, *rest):
    n_x = sz.n_row - 1
    outs, sem = rest[:-1], rest[-1]
    row = lax.axis_index("row")
    z = lax.axis_index("col")
    c = z * sz.n_depth + lax.axis_index("depth")

    def at(e):
        j, s = e // KB, e % KB
        k = c * sz.cols + j
        i = neighbour(near_ref, k, s)
        local = i - row * sz.rows
        return i, k, local, j, (local >= 0) & (local < sz.rows)

    def fetch(e, started):
        _, _, local, j, mine = at(e)

        @pl.when(mine)
        def _():
            pltpu.make_async_copy(block_at(matrix_ref, local, j), place(own_ref, e), sem).start()

        return started + mine.astype(jnp.int32)

    started = lax.fori_loop(0, sz.own, fetch, jnp.int32(0))

    def landed(_, carry):
        pltpu.make_async_copy(block_at(matrix_ref, 0, 0), place(own_ref, 0), sem).wait()
        return carry

    lax.fori_loop(0, started, landed, 0)

    first = jnp.maximum(row * sz.rows, c * sz.cols)
    last = jnp.minimum((row + 1) * sz.rows, (c + 1) * sz.cols)

    @pl.when(first < last)
    def _():
        down = lax.broadcasted_iota(jnp.int32, (BS, BS), 0)
        across = lax.broadcasted_iota(jnp.int32, (BS, BS), 1)
        count = min(sz.rows, sz.cols)
        for p in range(sz.pairs):
            d = first + 2 * p
            low = place(own_ref, (d - c * sz.cols) * KB + slot_of(near_ref, d, d))[...]
            if 2 * p + 1 < count:
                d = d + 1
                high = place(own_ref, (d - c * sz.cols) * KB + slot_of(near_ref, d, d))[...]
            else:
                high = jnp.zeros_like(low)
            both = jnp.where(down >= across, low, high)
            line = jnp.sum(jnp.where(down == across, high, 0.0), axis=0, keepdims=True)
            for out in outs:
                out[p * BS : (p + 1) * BS, :] = both
                out[out.shape[0] - 8 + p : out.shape[0] - 7 + p, :] = line

    def visit(e, carry):
        i, k, _, _, mine = at(e)

        @pl.when(mine & (i != k))
        def _():
            block = place(own_ref, e)[...]
            codes = []
            for m in range(1, sz.n_row):
                codes.append(code_at(table_ref, i, k, row ^ m, 0))
            for m in range(sz.n_col):
                codes.append(code_at(table_ref, i, k, z ^ m, sz.x_tables))
            for out, code in zip(outs, codes, strict=True):
                @pl.when(code != NONE)
                def _(out=out, code=code):
                    place(out, code)[...] = block

        return carry

    lax.fori_loop(0, sz.own, visit, 0)


def plan_kernel(sz, table_ref, near_ref, load_ref, job_ref, count_ref, zeros_ref, used_ref, blank_ref, sem):
    row = lax.axis_index("row")
    z = lax.axis_index("col")
    depth = lax.axis_index("depth")
    c = z * sz.n_depth + depth
    n_x, n_z = sz.n_row - 1, sz.n_col - 1

    blank_ref[...] = jnp.zeros_like(blank_ref)

    def wipe(i):
        return pltpu.make_async_copy(blank_ref, zeros_ref.at[pl.ds(pl.multiple_of(i * BS, BS), BS), :], sem)

    for i in range(sz.rows):
        wipe(i).start()

    def clear(e, carry):
        used_ref[e] = 0
        return carry

    lax.fori_loop(0, sz.n_a + sz.own, clear, 0)

    def find(e, n):
        local, j = e // sz.cols, e % sz.cols
        i, col = row * sz.rows + local, c * sz.cols + j
        kept = ((table_ref[0, i, col] >> PAT_BIT) & 1) == 1

        def search(n):
            start = n
            for s in range(KB):
                k = neighbour(near_ref, col, s)
                for t in range(KB):
                    hit = neighbour(near_ref, i, t) == k

                    @pl.when(hit)
                    def _(n=n, s=s, t=t):
                        job_ref[n, 0] = local * KB + t
                        job_ref[n, 1] = j * KB + s
                        job_ref[n, 2] = e
                        job_ref[n, 3] = (n == start).astype(jnp.int32)
                        used_ref[local * KB + t] = 1
                        used_ref[sz.n_a + j * KB + s] = 1

                    n = n + hit.astype(jnp.int32)

            @pl.when(n > start)
            def _():
                job_ref[n - 1, 3] = job_ref[n - 1, 3] + 2

            return n

        return lax.cond(kept, search, lambda n: n, n)

    count_ref[0] = lax.fori_loop(0, sz.n_out, find, jnp.int32(0))

    def add(n, source, code, dst, i, k, mine, sender_first):
        slot = jnp.where(mine, (k - c * sz.cols) * KB + slot_of(near_ref, k, i), code)
        packed = (i == k) & ~mine
        place_in = i - sender_first
        load_ref[n, 0] = jnp.where(mine, 0, source)
        load_ref[n, 1] = jnp.where(packed, place_in >> 1, slot)
        load_ref[n, 2] = jnp.where(packed, LOWER + (place_in & 1), PLAIN)
        load_ref[n, 3] = dst

    def load_a(e, n):
        local, t = e // KB, e % KB
        i = row * sz.rows + local
        k = neighbour(near_ref, i, t)

        @pl.when(used_ref[e] == 1)
        def _():
            kc = k // sz.cols
            m, q = (kc // sz.n_depth) ^ z, (kc % sz.n_depth) ^ depth
            across = 1 + n_x + n_z + (q - 1) * sz.n_col + m
            source = jnp.where(q == 0, n_x + m, across)
            code = code_at(table_ref, i, k, z, sz.x_tables)
            add(n, source, code, e, i, k, kc == c, jnp.maximum(row * sz.rows, kc * sz.cols))

        return n + used_ref[e]

    n = lax.fori_loop(0, sz.n_a, load_a, jnp.int32(0))

    def load_b(e, n):
        j, s = e // KB, e % KB
        col = c * sz.cols + j
        k = neighbour(near_ref, col, s)

        @pl.when(used_ref[sz.n_a + e] == 1)
        def _():
            kr = k // sz.rows
            code = code_at(table_ref, k, col, row, 0)
            add(n, kr ^ row, code, sz.n_a + e, k, col, kr == row, jnp.maximum(kr * sz.rows, c * sz.cols))

        return n + used_ref[sz.n_a + e]

    count_ref[1] = lax.fori_loop(0, sz.own, load_b, n)
    for i in range(sz.rows):
        wipe(i).wait()


def product_kernel(sz, load_ref, job_ref, count_ref, zeros_ref, *rest):
    del zeros_ref
    n_in = 1 + sz.n_row - 1 + sz.n_col - 1 + (sz.n_depth - 1) * sz.n_col
    sources = rest[:n_in]
    out_ref, high_ref, low_ref, acc_ref, sem = rest[n_in:]
    down = lax.broadcasted_iota(jnp.int32, (BS, BS), 0)
    across = lax.broadcasted_iota(jnp.int32, (BS, BS), 1)

    def load(n, carry):
        source, slot, kind, dst = (load_ref[n, f] for f in range(4))

        def keep(x):
            high = x.astype(jnp.bfloat16)
            place(high_ref, dst)[...] = high
            place(low_ref, dst)[...] = (x - high.astype(jnp.float32)).astype(jnp.bfloat16)

        for s, ref in enumerate(sources):
            @pl.when(source == s)
            def _(s=s, ref=ref):
                x = place(ref, slot)[...]
                if s == 0:
                    keep(x)
                    return

                @pl.when(kind == PLAIN)
                def _():
                    keep(x)

                @pl.when(kind == LOWER)
                def _():
                    keep(jnp.where(down >= across, x, x.T))

                @pl.when(kind == UPPER)
                def _():
                    line = ref[pl.ds(ref.shape[0] - 8 + slot, 1), :]
                    keep(jnp.where(down < across, x, jnp.where(down > across, x.T, line)))

        return carry

    lax.fori_loop(0, count_ref[1], load, 0)

    def multiply(n, stored):
        a, b, target, ends = (job_ref[n, f] for f in range(4))
        ah, al = place(high_ref, a)[...], place(low_ref, a)[...]
        bh, bl = place(high_ref, sz.n_a + b)[...], place(low_ref, sz.n_a + b)[...]
        dot = functools.partial(jnp.dot, preferred_element_type=jnp.float32)
        value = dot(ah, bh) + (dot(ah, bl) + dot(al, bh))
        acc = place(acc_ref, target)
        acc[...] = jnp.where((ends & 1) == 1, 0.0, acc[...]) + value

        @pl.when(ends >= 2)
        def _():
            pltpu.make_async_copy(acc, block_at(out_ref, target // sz.cols, target % sz.cols), sem).start()

        return stored + (ends >> 1)

    stored = lax.fori_loop(0, count_ref[0], multiply, jnp.int32(0))

    def written(_, carry):
        pltpu.make_async_copy(place(acc_ref, 0), block_at(out_ref, 0, 0), sem).wait()
        return carry

    lax.fori_loop(0, stored, written, 0)


def swaps(size, m):
    return [(i, i ^ m) for i in range(size)]


def exchange_and_multiply(sz, far, near, matrix, table, near_list):
    n_x, n_z = sz.n_row - 1, sz.n_col - 1
    smem = pl.BlockSpec(memory_space=pltpu.SMEM)
    vmem = pl.BlockSpec(memory_space=pltpu.VMEM)
    anywhere = pl.BlockSpec(memory_space=pl.ANY)

    def blocks(n):
        return jax.ShapeDtypeStruct((n * BS, BS), jnp.float32)

    far_shape = jax.ShapeDtypeStruct((far * BS + 8, BS), jnp.float32)
    near_shape = jax.ShapeDtypeStruct((near * BS + 8, BS), jnp.float32)
    own, *packed = pl.pallas_call(
        functools.partial(pack_kernel, sz),
        out_shape=[blocks(sz.own)] + [far_shape] * n_x + [near_shape] + [far_shape] * n_z,
        in_specs=[smem, smem, anywhere],
        out_specs=[vmem] * (2 + n_x + n_z),
        scratch_shapes=[pltpu.SemaphoreType.DMA],
        compiler_params=pltpu.CompilerParams(vmem_limit_bytes=32 * 2**20),
        name="pack",
    )(table, near_list, matrix)
    loads, jobs, counts, zeros = pl.pallas_call(
        functools.partial(plan_kernel, sz),
        out_shape=[
            jax.ShapeDtypeStruct((sz.n_a + sz.own, 4), jnp.int32),
            jax.ShapeDtypeStruct((sz.own * KB, 4), jnp.int32),
            jax.ShapeDtypeStruct((2,), jnp.int32),
            jax.ShapeDtypeStruct(matrix.shape, matrix.dtype),
        ],
        in_specs=[smem, smem],
        out_specs=[smem, smem, smem, anywhere],
        scratch_shapes=[
            pltpu.SMEM((sz.n_a + sz.own,), jnp.int32),
            pltpu.VMEM((BS, matrix.shape[1]), jnp.float32),
            pltpu.SemaphoreType.DMA,
        ],
        cost_estimate=pl.CostEstimate(flops=0, bytes_accessed=20_000_000, transcendentals=0),
        name="plan",
    )(table, near_list)
    zs = [lax.ppermute(packed[n_x + m], "col", swaps(sz.n_col, m)) for m in range(n_z, 0, -1)][::-1]
    xs = [lax.ppermute(packed[m - 1], "row", swaps(sz.n_row, m)) for m in range(n_x, 0, -1)][::-1]
    ds = []
    for q in range(1, sz.n_depth):
        for block_list in [packed[n_x]] + zs:
            ds.append(lax.ppermute(block_list, "depth", swaps(sz.n_depth, q)))
    sources = [own, *xs, *zs, *ds]
    return pl.pallas_call(
        functools.partial(product_kernel, sz),
        out_shape=jax.ShapeDtypeStruct(matrix.shape, matrix.dtype),
        in_specs=[smem] * 3 + [anywhere] + [vmem] * len(sources),
        out_specs=anywhere,
        input_output_aliases={3: 0},
        scratch_shapes=[
            pltpu.VMEM(((sz.n_a + sz.own) * BS, BS), jnp.bfloat16),
            pltpu.VMEM(((sz.n_a + sz.own) * BS, BS), jnp.bfloat16),
            pltpu.VMEM((sz.n_out * BS, BS), jnp.float32),
            pltpu.SemaphoreType.DMA,
        ],
        compiler_params=pltpu.CompilerParams(vmem_limit_bytes=40 * 2**20),
        name="product",
    )(loads, jobs, counts, zeros, *sources)


def shards(sz, matrix, occupancy, pattern):
    smem = pl.BlockSpec(memory_space=pltpu.SMEM)
    vmem = pl.BlockSpec(memory_space=pltpu.VMEM)
    table, near_list, bucket = pl.pallas_call(
        functools.partial(table_kernel, sz),
        out_shape=[
            jax.ShapeDtypeStruct((sz.tables, sz.nb, sz.nb), jnp.int32),
            jax.ShapeDtypeStruct((1, sz.nb), jnp.int32),
            jax.ShapeDtypeStruct((1,), jnp.int32),
        ],
        in_specs=[vmem, vmem],
        out_specs=[vmem, vmem, smem],
        name="tables",
    )(occupancy, pattern)
    branches = [functools.partial(exchange_and_multiply, sz, far, near) for far, near in sz.buckets]
    return lax.switch(bucket[0], branches, matrix, table, near_list)


def solution(mesh):
    def whole(matrix, occupancy, pattern):
        sz = Sizes(mesh, matrix.shape)
        return jax.shard_map(
            functools.partial(shards, sz),
            mesh=mesh,
            in_specs=(P("row", ("col", "depth")), P(), P()),
            out_specs=P("row", ("col", "depth")),
            check_vma=False,
        )(matrix, occupancy, pattern)

    return whole
```

time: 714 us -> 93.2 us (0.13)
  waiting for transfers between devices: 492 us -> 28.2 us
  matrix products: 183 us -> 0 us
  Pallas kernels: 0 us -> 32.5 us
  starting transfers between devices: 0.04 us -> 28.1 us
  local copies, waits for them, and re-layouts: 16.9 us -> 4.05 us
  between operations: 13.4 us -> 0.86 us
    all_gather x2 -> x0, waiting for transfers between devices: 491 us -> none  [the longest x1 325 us: shards(): left_panel = lax.all_gather(masked, ('col', 'depth'), axis=1, tiled=True)]
    dot_general x1 -> x0, matrix products: 183 us -> none  [shards(): jnp.dot(left_panel, lax.all_gather(masked, 'row', axis=0, tiled=True), pr...]
    pallas_call x0 -> x4, Pallas kernels: none -> 32.5 us  [the longest x1 14.1 us: exchange_and_multiply(): pl.pallas_call(functools.partial(plan_kernel, sz), out_shape=[jax.ShapeDt...]
    ppermute x0 -> x10, waiting for transfers between devices: none -> 28.2 us  [the longest x3 18.5 us: exchange_and_multiply(): lax.ppermute(packed[n_x + m], 'col', swaps(sz.n_col, m))]
    ppermute x0 -> x10, starting transfers between devices: none -> 28.1 us  [the longest x4 22.4 us: exchange_and_multiply(): ds.append(lax.ppermute(block_list, 'depth', swaps(sz.n_depth, q)))]
  transfers between devices with their start and end apart: 2 -> 10, of which waited for: 2 -> 4; matrix products, arithmetic and copies ran while one was open for 1% -> 0% of each run, Pallas kernels for 0% -> 15%
where the time goes in v1:
time: 93.2 us; the launch traced here: 94.3 us
  Pallas kernels  32.5 us (35%)
  waiting for transfers between devices  28.2 us (30%)
  starting transfers between devices  28.1 us (30%)
  local copies, waits for them, and re-layouts  4.05 us (4%)
    ppermute x4, starting transfers between devices, exchange_and_multiply(): ds.append(lax.ppermute(block_list, 'depth', swaps(sz.n_depth, q)))  22.4 us
    ppermute x3, waiting for transfers between devices, exchange_and_multiply(): lax.ppermute(packed[n_x + m], 'col', swaps(sz.n_col, m))  18.5 us
    pallas_call x1, Pallas kernels, exchange_and_multiply(): pl.pallas_call(functools.partial(plan_kernel, sz), out_shape=[jax.ShapeDt...  14.1 us
    pallas_call x1, Pallas kernels, exchange_and_multiply(): pl.pallas_call(functools.partial(product_kernel, sz), out_shape=jax.Shape...  10.8 us
    ppermute x3, waiting for transfers between devices, exchange_and_multiply(): lax.ppermute(packed[m - 1], 'row', swaps(sz.n_row, m))  9.62 us
    pallas_call x1, Pallas kernels, exchange_and_multiply(): pl.pallas_call(functools.partial(pack_kernel, sz), out_shape=[blocks(sz.o...  4.76 us
    cond x10, local copies, waits for them, and re-layouts  4.05 us
    ppermute x3, starting transfers between devices, exchange_and_multiply(): lax.ppermute(packed[n_x + m], 'col', swaps(sz.n_col, m))  3.06 us
  transfers between devices with their start and end apart: 10, of which 4 were waited for; matrix products, arithmetic and copies ran while one was open for 0% of the time, Pallas kernels for 15%

profile of v1, /device:TPU:11, one launch (start us, length us, event | category | flops | bytes accessed | tf_op | source)
XLA Modules:
  0.0 94.3 jit_solution(11341825382696427983)
XLA Ops:
  0.0 2.8 %tables.1 = (s32[2,48,48]{2,1,0:T(8,128)S(1)}, s32[1,48]{1,0:T(1,128)S(1)}, s32[1]{0:T(128)}) custom-call(s32[48,48]{1,0:T(8,128)} %occ_ref.1, s32[48,48]{1,0:T(8,128)} %pat_ref.1), custom_call_target="tpu_custom_call" | custom-call | tf_op jit(solution)/shard_map/tables/pallas_call | solution.py:440
  3.5 90.6 %conditional.1 = (f32[1536,768]{1,0:T(8,128)}) conditional(s32[]{:T(128)} %bitcast, (s32[2,48,48]{2,1,0:T(8,128)S(1)}, s32[1,48]{1,0:T(1,128)S(1)}, f32[1536,768]{1,0:T(8,128)}) %tuple.26, (s32[2,48,48]{2,1,0:T(8,128)S(1)}, s32[1,48]{1,0:T(1,128)S(1)}, f32[1536,768]{1,0:T(8,128)}) %tuple.26, ...), branch_computations={%region_0.0_spmd, %region_1.0_spmd, %region_2.0_spmd, %region_3.0_... | conditional | bytes 95672648 | solution.py:452
  3.5 4.8 %pack.11 = (f32[3072,128]{1,0:T(8,128)S(1)}, f32[1160,128]{1,0:T(8,128)S(1)}, f32[1160,128]{1,0:T(8,128)S(1)}, f32[1160,128]{1,0:T(8,128)}, f32[1800,128]{1,0:T(...) custom-call(s32[2,48,48]{2,1,0:T(8,128)S(1)} %get-tuple-element.115.table_ref, ...), custom_call_target="tpu_custom_call" | custom-call | tf_op jit(solution)/shard_map/cond/branch_4_fun/pack/pallas_call | solution.py:386
  8.3 0.7 collective-permute-start.40
  9.0 0.7 collective-permute-start.41
  9.7 0.3 collective-permute-start.43
  9.9 2.6 %collective-permute-start.44 = (f32[1160,128]{1,0:T(8,128)S(1)}, f32[1160,128]{1,0:T(8,128)}, u32[]{:S(2)}, u32[]{:S(2)}) collective-permute-start(f32[1160,128]{1,0:T(8,128)S(1)} %get-tuple-element.127), channel_id=1, source_target_pairs={{0,4},{2,6},{4,0},{6,2},{1,5},{3,7},{5,1},{7,3},{8,12},{10,14},{12... | collective-permute-start | bytes 1781768 | tf_op jit(solution)/shard_map/cond/branch_4_fun/ppermute | solution.py:413
  12.6 0.1 collective-permute-start.45
  12.7 9.6 %collective-permute-done.40.rest_1_ = f32[1160,128]{1,0:T(8,128)S(1)} collective-permute-done((f32[1160,128]{1,0:T(8,128)S(1)}, f32[1160,128]{1,0:T(8,128)S(1)}, u32[]{:S(2)}, u32[]{:S(2)}) %collective-permute-start.40) | collective-permute-done | bytes 593952 | tf_op jit(solution)/shard_map/cond/branch_4_fun/ppermute | solution.py:414
  22.3 1.9 %collective-permute-start.46 = (f32[1800,128]{1,0:T(8,128)}, f32[1800,128]{1,0:T(8,128)S(1)}, u32[]{:S(2)}, u32[]{:S(2)}) collective-permute-start(f32[1800,128]{1,0:T(8,128)} %get-tuple-element.129), channel_id=1, source_target_pairs={{0,1},{1,0},{2,3},{3,2},{4,5},{5,4},{6,7},{7,6},{8,9},{9,8},{10,11... | collective-permute-start | bytes 2764808 | tf_op jit(solution)/shard_map/cond/branch_4_fun/ppermute | solution.py:418
  24.2 0.0 collective-permute-done.41.rest_2_
  24.2 0.0 copy-start.4
  24.2 0.8 copy-done.4
  25.0 1.3 %collective-permute-start.42 = (f32[1160,128]{1,0:T(8,128)}, f32[1160,128]{1,0:T(8,128)}, u32[]{:S(2)}, u32[]{:S(2)}) collective-permute-start(f32[1160,128]{1,0:T(8,128)} %get-tuple-element.125), channel_id=1, source_target_pairs={{0,24},{8,16},{16,8},{24,0},{1,25},{9,17},{17,9},{25,1},{2,26},{10... | collective-permute-start | bytes 1781768 | tf_op jit(solution)/shard_map/cond/branch_4_fun/ppermute | solution.py:414
  26.3 7.1 %collective-permute-done.43.rest_4_ = f32[1160,128]{1,0:T(8,128)} collective-permute-done((f32[1160,128]{1,0:T(8,128)S(1)}, f32[1160,128]{1,0:T(8,128)}, u32[]{:S(2)}, u32[]{:S(2)}) %collective-permute-start.43) | collective-permute-done | bytes 593952 | tf_op jit(solution)/shard_map/cond/branch_4_fun/ppermute | solution.py:413
  33.5 1.9 %collective-permute-start.47 = (f32[1160,128]{1,0:T(8,128)}, f32[1160,128]{1,0:T(8,128)}, u32[]{:S(2)}, u32[]{:S(2)}) collective-permute-start(f32[1160,128]{1,0:T(8,128)} %collective-permute-done.43.rest_4_), channel_id=1, source_target_pairs={{0,1},{1,0},{2,3},{3,2},{4,5},{5,4},{6,7},{7,6},{8,9},{9,8},{10,11... | collective-permute-start | bytes 1781768 | tf_op jit(solution)/shard_map/cond/branch_4_fun/ppermute | solution.py:418
  35.3 2.1 %collective-permute-done.44.rest_5_ = f32[1160,128]{1,0:T(8,128)} collective-permute-done((f32[1160,128]{1,0:T(8,128)S(1)}, f32[1160,128]{1,0:T(8,128)}, u32[]{:S(2)}, u32[]{:S(2)}) %collective-permute-start.44) | collective-permute-done | bytes 593952 | tf_op jit(solution)/shard_map/cond/branch_4_fun/ppermute | solution.py:413
  37.4 16.5 %collective-permute-start.48 = (f32[1160,128]{1,0:T(8,128)}, f32[1160,128]{1,0:T(8,128)}, u32[]{:S(2)}, u32[]{:S(2)}) collective-permute-start(f32[1160,128]{1,0:T(8,128)} %collective-permute-done.44.rest_5_), channel_id=1, source_target_pairs={{0,1},{1,0},{2,3},{3,2},{4,5},{5,4},{6,7},{7,6},{8,9},{9,8},{10,11... | collective-permute-start | bytes 1781768 | tf_op jit(solution)/shard_map/cond/branch_4_fun/ppermute | solution.py:418
  53.9 9.3 %collective-permute-done.45.rest_6_ = f32[1160,128]{1,0:T(8,128)} collective-permute-done((f32[1160,128]{1,0:T(8,128)S(1)}, f32[1160,128]{1,0:T(8,128)}, u32[]{:S(2)}, u32[]{:S(2)}) %collective-permute-start.45) | collective-permute-done | bytes 593952 | tf_op jit(solution)/shard_map/cond/branch_4_fun/ppermute | solution.py:413
  63.2 2.2 %collective-permute-start.49 = (f32[1160,128]{1,0:T(8,128)}, f32[1160,128]{1,0:T(8,128)}, u32[]{:S(2)}, u32[]{:S(2)}) collective-permute-start(f32[1160,128]{1,0:T(8,128)} %collective-permute-done.45.rest_6_), channel_id=1, source_target_pairs={{0,1},{1,0},{2,3},{3,2},{4,5},{5,4},{6,7},{7,6},{8,9},{9,8},{10,11... | collective-permute-start | bytes 1781768 | tf_op jit(solution)/shard_map/cond/branch_4_fun/ppermute | solution.py:418
  65.4 14.1 %plan.11 = (s32[72,4]{1,0:T(8,128)}, s32[96,4]{1,0:T(8,128)}, s32[2]{0:T(128)}, f32[1536,768]{1,0:T(8,128)}) custom-call(s32[2,48,48]{2,1,0:T(8,128)S(1)} %get-tuple-element.115.table_ref, s32[1,48]{1,0:T(1,128)S(1)} %get-tuple-element.116.near_ref), custom_call_target="tpu_custom_call" | custom-call | bytes 20000000 | tf_op jit(solution)/shard_map/cond/branch_4_fun/plan/pallas_call | solution.py:395
  79.5 0.0 collective-permute-done.42.rest_3_
  79.5 0.0 collective-permute-done.46.rest_7_
  79.5 0.0 collective-permute-done.47.rest_8_
  79.5 0.0 collective-permute-done.48.rest_9_
  79.5 0.0 collective-permute-done.49.rest_10_
  79.6 0.0 copy-start.5
  79.6 1.1 %copy-done.5 = f32[1160,128]{1,0:T(8,128)S(1)} copy-done((f32[1160,128]{1,0:T(8,128)S(1)}, f32[1160,128]{1,0:T(8,128)}, u32[]{:S(2)}) %copy-start.5) | copy-done | bytes 593944 | tf_op jit(solution)/shard_map/cond
  80.6 0.8 copy-done.6
  81.4 0.8 copy-done.14
  82.2 0.6 copy-done.25
  82.8 10.8 %product.11 = f32[1536,768]{1,0:T(8,128)} custom-call(s32[72,4]{1,0:T(8,128)S(1)} %copy-done.14, s32[96,4]{1,0:T(8,128)S(1)} %copy-done.6, s32[2]{0:T(128)S(1)} %copy-done.25, f32[1536,768]{1,0:T(8,128)} %get-tuple-element.120.zeros_ref, f32[3072,128]{1,0:T(8,128)S(1)} %get-tuple-element.122.rest_0_, ...), custom_call_target="tpu_custom_call", output_to_operand_aliasing={{}: (3, {})} | custom-call | tf_op jit(solution)/shard_map/cond/branch_4_fun/product/pallas_call | solution.py:420
  (3 shorter events, 0.0 us)
Async XLA Ops:
  8.3 14.0 %collective-permute-start.40 = (f32[1160,128]{1,0:T(8,128)S(1)}, f32[1160,128]{1,0:T(8,128)S(1)}, u32[]{:S(2)}, u32[]{:S(2)}) collective-permute-start(f32[1160,128]{1,0:T(8,128)S(1)} %get-tuple-element.123), channel_id=1, source_target_pairs={{0,8},{8,0},{16,24},{24,16},{1,9},{9,1},{17,25},{25,17},{2,10},{10... | collective-permute-start | bytes 1781768 | tf_op jit(solution)/shard_map/cond/branch_4_fun/ppermute | solution.py:414
  9.0 15.2 %collective-permute-start.41 = (f32[1160,128]{1,0:T(8,128)S(1)}, f32[1160,128]{1,0:T(8,128)S(1)}, u32[]{:S(2)}, u32[]{:S(2)}) collective-permute-start(f32[1160,128]{1,0:T(8,128)S(1)} %get-tuple-element.124), channel_id=1, source_target_pairs={{0,16},{8,24},{16,0},{24,8},{1,17},{9,25},{17,1},{25,9},{2,18},{10... | collective-permute-start | bytes 1781768 | tf_op jit(solution)/shard_map/cond/branch_4_fun/ppermute | solution.py:414
  9.7 23.8 %collective-permute-start.43 = (f32[1160,128]{1,0:T(8,128)S(1)}, f32[1160,128]{1,0:T(8,128)}, u32[]{:S(2)}, u32[]{:S(2)}) collective-permute-start(f32[1160,128]{1,0:T(8,128)S(1)} %get-tuple-element.126), channel_id=1, source_target_pairs={{0,2},{2,0},{4,6},{6,4},{1,3},{3,1},{5,7},{7,5},{8,10},{10,8},{12,... | collective-permute-start | bytes 1781768 | tf_op jit(solution)/shard_map/cond/branch_4_fun/ppermute | solution.py:413
  9.9 27.5 %collective-permute-start.44 = (f32[1160,128]{1,0:T(8,128)S(1)}, f32[1160,128]{1,0:T(8,128)}, u32[]{:S(2)}, u32[]{:S(2)}) collective-permute-start(f32[1160,128]{1,0:T(8,128)S(1)} %get-tuple-element.127), channel_id=1, source_target_pairs={{0,4},{2,6},{4,0},{6,2},{1,5},{3,7},{5,1},{7,3},{8,12},{10,14},{12... | collective-permute-start | bytes 1781768 | tf_op jit(solution)/shard_map/cond/branch_4_fun/ppermute | solution.py:413
  12.6 50.6 %collective-permute-start.45 = (f32[1160,128]{1,0:T(8,128)S(1)}, f32[1160,128]{1,0:T(8,128)}, u32[]{:S(2)}, u32[]{:S(2)}) collective-permute-start(f32[1160,128]{1,0:T(8,128)S(1)} %get-tuple-element.128), channel_id=1, source_target_pairs={{0,6},{2,4},{4,2},{6,0},{1,7},{3,5},{5,3},{7,1},{8,14},{10,12},{12... | collective-permute-start | bytes 1781768 | tf_op jit(solution)/shard_map/cond/branch_4_fun/ppermute | solution.py:413
  22.3 57.2 %collective-permute-start.46 = (f32[1800,128]{1,0:T(8,128)}, f32[1800,128]{1,0:T(8,128)S(1)}, u32[]{:S(2)}, u32[]{:S(2)}) collective-permute-start(f32[1800,128]{1,0:T(8,128)} %get-tuple-element.129), channel_id=1, source_target_pairs={{0,1},{1,0},{2,3},{3,2},{4,5},{5,4},{6,7},{7,6},{8,9},{9,8},{10,11... | collective-permute-start | bytes 2764808 | tf_op jit(solution)/shard_map/cond/branch_4_fun/ppermute | solution.py:418
  24.2 0.8 copy-start.4
  25.0 54.5 %collective-permute-start.42 = (f32[1160,128]{1,0:T(8,128)}, f32[1160,128]{1,0:T(8,128)}, u32[]{:S(2)}, u32[]{:S(2)}) collective-permute-start(f32[1160,128]{1,0:T(8,128)} %get-tuple-element.125), channel_id=1, source_target_pairs={{0,24},{8,16},{16,8},{24,0},{1,25},{9,17},{17,9},{25,1},{2,26},{10... | collective-permute-start | bytes 1781768 | tf_op jit(solution)/shard_map/cond/branch_4_fun/ppermute | solution.py:414
  33.5 46.1 %collective-permute-start.47 = (f32[1160,128]{1,0:T(8,128)}, f32[1160,128]{1,0:T(8,128)}, u32[]{:S(2)}, u32[]{:S(2)}) collective-permute-start(f32[1160,128]{1,0:T(8,128)} %collective-permute-done.43.rest_4_), channel_id=1, source_target_pairs={{0,1},{1,0},{2,3},{3,2},{4,5},{5,4},{6,7},{7,6},{8,9},{9,8},{10,11... | collective-permute-start | bytes 1781768 | tf_op jit(solution)/shard_map/cond/branch_4_fun/ppermute | solution.py:418
  37.4 42.1 %collective-permute-start.48 = (f32[1160,128]{1,0:T(8,128)}, f32[1160,128]{1,0:T(8,128)}, u32[]{:S(2)}, u32[]{:S(2)}) collective-permute-start(f32[1160,128]{1,0:T(8,128)} %collective-permute-done.44.rest_5_), channel_id=1, source_target_pairs={{0,1},{1,0},{2,3},{3,2},{4,5},{5,4},{6,7},{7,6},{8,9},{9,8},{10,11... | collective-permute-start | bytes 1781768 | tf_op jit(solution)/shard_map/cond/branch_4_fun/ppermute | solution.py:418
  63.2 16.3 %collective-permute-start.49 = (f32[1160,128]{1,0:T(8,128)}, f32[1160,128]{1,0:T(8,128)}, u32[]{:S(2)}, u32[]{:S(2)}) collective-permute-start(f32[1160,128]{1,0:T(8,128)} %collective-permute-done.45.rest_6_), channel_id=1, source_target_pairs={{0,1},{1,0},{2,3},{3,2},{4,5},{5,4},{6,7},{7,6},{8,9},{9,8},{10,11... | collective-permute-start | bytes 1781768 | tf_op jit(solution)/shard_map/cond/branch_4_fun/ppermute | solution.py:418
  79.6 1.1 %copy-start.5 = (f32[1160,128]{1,0:T(8,128)S(1)}, f32[1160,128]{1,0:T(8,128)}, u32[]{:S(2)}) copy-start(f32[1160,128]{1,0:T(8,128)} %copy-done.4) | copy-start | bytes 1781764 | tf_op jit(solution)/shard_map/cond
  80.6 0.8 copy-start.6
  81.4 0.8 copy-start.14
  82.2 0.6 copy-start.25

commit v2 on v0

v2 whole, which is shorter than its diff:
```python
import functools

import jax
import jax.numpy as jnp
from jax import lax
from jax.experimental import pallas as pl
from jax.experimental.pallas import tpu as pltpu
from jax.sharding import PartitionSpec as P

BS = 128
KB = 4
NONE = 31
GROUP = 6
PAT_BIT = 30
PLAIN, LOWER, UPPER = 0, 1, 2
UNROLL = 4


class Sizes:
    def __init__(self, mesh, matrix_shape):
        self.n_row = mesh.shape["row"]
        self.n_col = mesh.shape["col"]
        self.n_depth = mesh.shape["depth"]
        self.nb = matrix_shape[0] // BS
        self.rows = self.nb // self.n_row
        self.cols = self.nb // (self.n_col * self.n_depth)
        self.pairs = (min(self.rows, self.cols) + 1) // 2
        self.own = KB * self.cols
        self.n_a = KB * self.rows
        self.n_load = self.n_a + self.own
        self.n_job = self.own * KB
        self.n_out = self.rows * self.cols
        self.cap = KB * min(self.rows, self.cols)
        self.stages = 2
        self.jobs_at = self.stages * self.n_load
        self.targets_at = self.jobs_at + self.stages * (self.n_job + UNROLL)
        self.counts_at = self.targets_at + self.n_out
        self.n_plan = self.counts_at + 2 * self.stages + 1
        self.x_tables = -(-self.n_row // GROUP)
        self.tables = self.x_tables + -(-self.n_col // GROUP)
        self.block = self.n_col
        self.lengths = []
        for far in (5, 6, 7, 8, 9, 10, 12):
            if far + 5 < self.cap:
                self.lengths.append((far, far + 1, far + 2, far + 5))
        self.lengths.append((self.cap,) * 4)


def group_of(place, size, count):
    group = jnp.zeros_like(place)
    for g in range(1, count):
        group = group + (place >= g * size).astype(jnp.int32)
    return group


def ones_dot(a, b):
    return jnp.dot(a.astype(jnp.bfloat16), b.astype(jnp.bfloat16), preferred_element_type=jnp.float32)


def table_kernel(sz, occ_ref, pat_ref, table_ref, near_ref, bucket_ref):
    nb = sz.nb
    occ = (occ_ref[...] != 0).astype(jnp.float32)
    pat = (pat_ref[...] != 0).astype(jnp.float32)
    row_i = lax.broadcasted_iota(jnp.int32, (nb, nb), 0)
    col_i = lax.broadcasted_iota(jnp.int32, (nb, nb), 1)
    off = jnp.where(row_i == col_i, 0.0, occ)
    row_rg = group_of(row_i, sz.rows, sz.n_row)
    col_rg = group_of(col_i, sz.rows, sz.n_row)
    row_cg = group_of(row_i, sz.cols, sz.n_col * sz.n_depth)
    col_cg = group_of(col_i, sz.cols, sz.n_col * sz.n_depth)
    col_zg = group_of(col_i, sz.cols * sz.n_depth, sz.n_col)
    same = row_cg == col_cg
    before = (same & (row_i < col_i)).astype(jnp.float32)
    same = same.astype(jnp.float32)
    above = ((row_rg == col_rg) & (col_i < row_i)).astype(jnp.float32)
    first = jnp.maximum(row_rg * sz.rows, col_cg * sz.cols)
    last = jnp.minimum((row_rg + 1) * sz.rows, (col_cg + 1) * sz.cols)
    skip = jnp.where(first < last, sz.pairs, 0)

    def codes(need, sent):
        listed = jnp.where(need > 0, off, 0.0)
        rank = ones_dot(listed, before) + ones_dot(above, ones_dot(listed, same))
        rank = rank.astype(jnp.int32) + skip
        used = jnp.where(listed > 0, rank + 1, skip)
        return jnp.where(listed > 0, jnp.minimum(rank, NONE - 1), NONE), jnp.where(sent, used, 0), jnp.where(sent, 0, used)

    most = [jnp.zeros((nb, nb), jnp.int32) for _ in range(4)]
    tables = [jnp.zeros((nb, nb), jnp.int32) for _ in range(sz.tables)]
    for r in range(sz.n_row):
        need = ones_dot(jnp.where(col_rg == r, occ, 0.0), pat)
        code, count, _ = codes(need, row_rg != r)
        most[2] = jnp.maximum(most[2], count)
        tables[r // GROUP] += code << (5 * (r % GROUP))
    for z in range(sz.n_col):
        need = ones_dot(jnp.where(col_zg == z, pat, 0.0), occ)
        code, count, here = codes(need, col_zg != z)
        side = col_zg == (z ^ 1)
        most[0] = jnp.maximum(most[0], jnp.where(side, 0, count))
        most[1] = jnp.maximum(most[1], jnp.where(side, count, 0))
        most[3] = jnp.maximum(most[3], here)
        tables[sz.x_tables + z // GROUP] += code << (5 * (z % GROUP))
    tables[0] += pat.astype(jnp.int32) << PAT_BIT
    for t in range(sz.tables):
        table_ref[t] = tables[t]

    lower = (col_i < row_i).astype(jnp.float32)
    order = ones_dot(lower, occ).astype(jnp.int32)
    weight = jnp.where(occ > 0, row_i << (6 * jnp.minimum(order, KB - 1)), 0)
    near_ref[...] = jnp.sum(weight, axis=0, keepdims=True)
    bucket = jnp.zeros((nb, nb), jnp.int32)
    for lengths in sz.lengths[:-1]:
        over = most[0] > lengths[0]
        for count, length in zip(most[1:], lengths[1:], strict=True):
            over = over | (count > length)
        bucket = bucket + over.astype(jnp.int32)
    bucket_ref[0] = jnp.max(bucket)


def neighbour(near_ref, block, s):
    return (near_ref[0, block] >> (6 * s)) & 63


def slot_of(near_ref, block, other):
    slot = jnp.int32(0)
    for u in range(KB):
        slot = slot + (neighbour(near_ref, block, u) < other).astype(jnp.int32)
    return slot


def code_at(table_ref, i, k, group, base):
    word = table_ref[base + group // GROUP, i, k]
    return (word >> (5 * (group % GROUP))) & 31


def place(ref, slot):
    return ref.at[pl.ds(pl.multiple_of(slot * BS, BS), BS), :]


def block_at(ref, i, j):
    return ref.at[pl.ds(pl.multiple_of(i * BS, BS), BS), pl.ds(pl.multiple_of(j * BS, BS), BS)]


def own_slot(sz, near_ref, i, k, c):
    return (k - c * sz.cols) * KB + slot_of(near_ref, k, i)


def repeat(first, last, body):
    def step(n, carry):
        body(n)
        return carry

    lax.fori_loop(first, last, step, 0)


def pack_kernel(sz, table_ref, near_ref, matrix_ref, own_ref, *rest):
    outs, sems = rest[:-1], rest[-1]
    row = lax.axis_index("row")
    z = lax.axis_index("col")
    c = z * sz.n_depth + lax.axis_index("depth")

    def at(e):
        k = c * sz.cols + e // KB
        i = neighbour(near_ref, k, e % KB)
        return i, k, (i >= row * sz.rows) & (i < (row + 1) * sz.rows)

    def fetching(e, i):
        block = block_at(matrix_ref, jnp.clip(i - row * sz.rows, 0, sz.rows - 1), e // KB)
        return pltpu.make_async_copy(block, place(own_ref, e), sems.at[e])

    def fetch(e):
        i, _, mine = at(e)

        @pl.when(mine)
        def _():
            fetching(e, i).start()

    repeat(0, sz.own, fetch)

    codes = [(sz.x_tables, z ^ m) for m in range(sz.n_col)] + [(0, row ^ m) for m in range(1, sz.n_row)]

    def visit(e):
        i, k, mine = at(e)

        @pl.when(mine)
        def _():
            fetching(e, i).wait()

        @pl.when(mine & (i != k))
        def _():
            block = place(own_ref, e)[...]
            for out, (base, group) in zip(outs, codes, strict=True):
                code = code_at(table_ref, i, k, group, base)

                @pl.when(code != NONE)
                def _(out=out, code=code):
                    place(out, code)[...] = block

    repeat(0, sz.own, visit)

    first = jnp.maximum(row * sz.rows, c * sz.cols)
    last = jnp.minimum((row + 1) * sz.rows, (c + 1) * sz.cols)

    @pl.when(first < last)
    def _():
        down = lax.broadcasted_iota(jnp.int32, (BS, BS), 0)
        across = lax.broadcasted_iota(jnp.int32, (BS, BS), 1)
        for p in range(sz.pairs):
            d = first + 2 * p
            low = place(own_ref, own_slot(sz, near_ref, d, d, c))[...]
            if 2 * p + 1 < min(sz.rows, sz.cols):
                high = place(own_ref, own_slot(sz, near_ref, d + 1, d + 1, c))[...]
            else:
                high = jnp.zeros_like(low)
            both = jnp.where(down >= across, low, high)
            line = jnp.sum(jnp.where(down == across, high, 0.0), axis=0, keepdims=True)
            for out in outs:
                out[p * BS : (p + 1) * BS, :] = both
                out[out.shape[0] - 8 + p : out.shape[0] - 7 + p, :] = line


def plan_kernel(sz, table_ref, near_ref, plan_ref, zeros_ref, slot_ref, seen_ref, blank_ref, sem):
    row = lax.axis_index("row")
    z = lax.axis_index("col")
    depth = lax.axis_index("depth")
    c = z * sz.n_depth + depth
    n_x = sz.n_row - 1

    blank_ref[...] = jnp.zeros_like(blank_ref)

    def wipe(i):
        return pltpu.make_async_copy(blank_ref, zeros_ref.at[pl.ds(pl.multiple_of(i * BS, BS), BS), :], sem)

    for i in range(sz.rows):
        wipe(i).start()

    def clear(ref, size):
        def step(e, carry):
            ref[e] = 0
            return carry

        lax.fori_loop(0, size, step, 0)

    clear(slot_ref, sz.n_load)
    clear(seen_ref, sz.n_out)

    def stage_of(k):
        kc = k // sz.cols
        kz = kc // sz.n_depth
        near = (kc % sz.n_depth == depth) & (kz >> 1 == z >> 1)
        return jnp.where(near, 0, 1)

    def count(counts, stage):
        return tuple(n + (stage == q).astype(jnp.int32) for q, n in enumerate(counts))

    def spot(counts, stage, size):
        n = counts[0]
        for q in range(1, sz.stages):
            n = jnp.where(stage == q, counts[q], n)
        return n + stage * size

    def find(e, carry):
        j, s = e // KB, e % KB
        col = c * sz.cols + j
        k = neighbour(near_ref, col, s)
        stage = stage_of(k)
        for t in range(KB):
            i = neighbour(near_ref, k, t)
            local = i - row * sz.rows
            mine = (local >= 0) & (local < sz.rows)
            kept = mine & (((table_ref[0, i, col] >> PAT_BIT) & 1) == 1)

            def add(carry, i=i, local=local):
                counts, targets = carry
                a = local * KB + slot_of(near_ref, i, k)
                target = local * sz.cols + j
                known = seen_ref[target]
                at = sz.jobs_at + spot(counts, stage, sz.n_job + UNROLL)
                plan_ref[at] = a + (e << 8) + (target << 16)
                slot_ref[a] = 1
                slot_ref[sz.n_a + e] = 1
                seen_ref[target] = 1

                @pl.when(known == 0)
                def _():
                    plan_ref[sz.targets_at + targets] = target

                return count(counts, stage), targets + 1 - known

            carry = lax.cond(kept, add, lambda carry: carry, carry)
        return carry

    none = (jnp.int32(0),) * sz.stages
    jobs, n_targets = lax.fori_loop(0, sz.own, find, (none, jnp.int32(0)))
    for q in range(sz.stages):
        for u in range(UNROLL):
            plan_ref[sz.jobs_at + q * (sz.n_job + UNROLL) + jobs[q] + u] = sz.n_out << 16

    def add(n, source, code, dst, i, k, mine, sender_first):
        slot = jnp.where(mine, own_slot(sz, near_ref, i, k, c), code)
        packed = (i == k) & ~mine
        order = i - sender_first
        source = jnp.where(mine, 0, source)
        slot = jnp.where(packed, order >> 1, slot)
        kind = jnp.where(packed, LOWER + (order & 1), PLAIN)
        plan_ref[n] = source + (slot << 8) + (kind << 16) + (dst << 18)

    def load_b(e, counts):
        j, s = e // KB, e % KB
        col = c * sz.cols + j

        def take(counts):
            k = neighbour(near_ref, col, s)
            kr = k // sz.rows
            code = code_at(table_ref, k, col, row, 0)
            sender = jnp.maximum(kr * sz.rows, c * sz.cols)
            add(counts[0], kr ^ row, code, sz.n_a + e, k, col, kr == row, sender)
            return count(counts, jnp.int32(0))

        return lax.cond(slot_ref[sz.n_a + e] == 1, take, lambda counts: counts, counts)

    def load_a(e, counts):
        local, t = e // KB, e % KB
        i = row * sz.rows + local

        def take(counts):
            k = neighbour(near_ref, i, t)
            kc = k // sz.cols
            kz, kd = kc // sz.n_depth, kc % sz.n_depth
            q = kd ^ depth
            stage = stage_of(k)
            code = code_at(table_ref, i, k, z, sz.x_tables)
            source = 1 + n_x + q * sz.block + (kz ^ z) - 1
            add(spot(counts, stage, sz.n_load), source, code, e, i, k, kc == c, jnp.maximum(row * sz.rows, kc * sz.cols))
            return count(counts, stage)

        return lax.cond(slot_ref[e] == 1, take, lambda counts: counts, counts)

    loads = lax.fori_loop(0, sz.own, load_b, none)
    loads = lax.fori_loop(0, sz.n_a, load_a, loads)
    for q in range(sz.stages):
        plan_ref[sz.counts_at + 2 * q] = loads[q]
        plan_ref[sz.counts_at + 2 * q + 1] = (jobs[q] + UNROLL - 1) // UNROLL
    plan_ref[sz.counts_at + 2 * sz.stages] = n_targets
    for i in range(sz.rows):
        wipe(i).wait()


def load_block(word, sources, a_ref, b_ref, n_a):
    source, slot, kind, dst = word & 255, (word >> 8) & 255, (word >> 16) & 3, word >> 18

    def keep(x):
        high = x.astype(jnp.bfloat16)
        low = (x - high.astype(jnp.float32)).astype(jnp.bfloat16)
        if b_ref is None:
            a_out = place(a_ref, dst)
            a_out[:, :BS], a_out[:, BS : 2 * BS], a_out[:, 2 * BS :] = high, low, high
            return

        @pl.when(dst < n_a)
        def _():
            a_out = place(a_ref, dst)
            a_out[:, :BS], a_out[:, BS : 2 * BS], a_out[:, 2 * BS :] = high, low, high

        @pl.when(dst >= n_a)
        def _():
            for p, part in enumerate((high, high, low)):
                place(b_ref, 3 * (dst - n_a) + p)[...] = part

    for s, ref in sources:
        @pl.when(source == s)
        def _(s=s, ref=ref):
            x = place(ref, slot)[...]
            if s == 0:
                keep(x)
                return

            @pl.when(kind == PLAIN)
            def _():
                keep(x)

            @pl.when(kind != PLAIN)
            def _():
                down = lax.broadcasted_iota(jnp.int32, (BS, BS), 0)
                across = lax.broadcasted_iota(jnp.int32, (BS, BS), 1)
                lower = kind == LOWER
                line = ref[pl.ds(ref.shape[0] - 8 + slot, 1), :]
                stored = (down > across) == lower
                edge = jnp.where(lower, x, line)
                keep(jnp.where(down == across, edge, jnp.where(stored, x, x.T)))


def run_stage(sz, stage, plan_ref, sources, a_ref, b_new_ref, b_ref, acc_ref):
    first = stage * sz.n_load
    repeat(
        first,
        first + plan_ref[sz.counts_at + 2 * stage],
        lambda n: load_block(plan_ref[n], sources, a_ref, b_new_ref, sz.n_a),
    )
    jobs = sz.jobs_at + stage * (sz.n_job + UNROLL)

    def multiply(n):
        words = [plan_ref[jobs + UNROLL * n + u] for u in range(UNROLL)]
        values = []
        for word in words:
            left = place(a_ref, word & 255)[...]
            b = pl.multiple_of(((word >> 8) & 255) * (3 * BS), 3 * BS)
            right = b_ref[pl.ds(b, 3 * BS), :]
            values.append(jnp.dot(left, right, preferred_element_type=jnp.float32))
        for word, value in zip(words, values, strict=True):
            place(acc_ref, word >> 16)[...] += value

    repeat(0, plan_ref[sz.counts_at + 2 * stage + 1], multiply)


def early_kernel(sz, numbers, plan_ref, *rest):
    sources = list(zip(numbers, rest[:-3], strict=True))
    b_ref, acc_ref, a_ref = rest[-3:]
    acc_ref[...] = jnp.zeros_like(acc_ref)
    run_stage(sz, 0, plan_ref, sources, a_ref, b_ref, b_ref, acc_ref)


def carry_on(sz, plan_ref, before_ref, acc_ref):
    def copy(n):
        target = plan_ref[sz.targets_at + n]
        place(acc_ref, target)[...] = place(before_ref, target)[...]

    repeat(0, plan_ref[sz.counts_at + 2 * sz.stages], copy)


def late_kernel(sz, numbers, plan_ref, zeros_ref, b_ref, before_ref, *rest):
    del zeros_ref
    sources = list(zip(numbers, rest[:-4], strict=True))
    out_ref, a_ref, acc_ref, sem = rest[-4:]
    carry_on(sz, plan_ref, before_ref, acc_ref)
    run_stage(sz, 1, plan_ref, sources, a_ref, None, b_ref, acc_ref)

    def store(n):
        target = plan_ref[sz.targets_at + n]
        pltpu.make_async_copy(place(acc_ref, target), block_at(out_ref, target // sz.cols, target % sz.cols), sem).start()

    n_targets = plan_ref[sz.counts_at + 2 * sz.stages]
    repeat(0, n_targets, store)
    repeat(0, n_targets, lambda n: pltpu.make_async_copy(place(acc_ref, 0), block_at(out_ref, 0, 0), sem).wait())


def swaps(size, m):
    return [(i, i ^ m) for i in range(size)]


def exchange_and_multiply(sz, lengths, matrix, table, near_list):
    n_x = sz.n_row - 1
    far_length, side_length, row_length, near_length = lengths
    smem = pl.BlockSpec(memory_space=pltpu.SMEM)
    vmem = pl.BlockSpec(memory_space=pltpu.VMEM)
    anywhere = pl.BlockSpec(memory_space=pltpu.HBM)
    params = pltpu.CompilerParams(vmem_limit_bytes=(24 if far_length < sz.cap else 44) * 2**20)
    small = pl.CostEstimate(flops=0, bytes_accessed=1024, transcendentals=0)

    def blocks(n):
        return jax.ShapeDtypeStruct((n * BS + 8, BS), jnp.float32)

    shapes = [jax.ShapeDtypeStruct((sz.own * BS, BS), jnp.float32), blocks(near_length), blocks(side_length)]
    shapes += [blocks(far_length)] * (sz.n_col - 2) + [blocks(row_length)] * n_x
    own, near, *lists = pl.pallas_call(
        functools.partial(pack_kernel, sz),
        out_shape=shapes,
        in_specs=[smem, smem, anywhere],
        out_specs=[vmem] * len(shapes),
        scratch_shapes=[pltpu.SemaphoreType.DMA((sz.own,))],
        compiler_params=params,
        cost_estimate=small,
        name="pack",
    )(table, near_list, matrix)
    zs = [lax.ppermute(x, "col", swaps(sz.n_col, m + 1)) for m, x in enumerate(lists[: sz.n_col - 1])]
    xs = [lax.ppermute(x, "row", swaps(sz.n_row, m + 1)) for m, x in enumerate(lists[sz.n_col - 1 :])]
    plan, zeros = pl.pallas_call(
        functools.partial(plan_kernel, sz),
        out_shape=[jax.ShapeDtypeStruct((sz.n_plan,), jnp.int32), jax.ShapeDtypeStruct(matrix.shape, matrix.dtype)],
        in_specs=[smem, smem],
        out_specs=[smem, anywhere],
        scratch_shapes=[
            pltpu.SMEM((sz.n_load,), jnp.int32),
            pltpu.SMEM((sz.n_out,), jnp.int32),
            pltpu.VMEM((BS, matrix.shape[1]), jnp.float32),
            pltpu.SemaphoreType.DMA,
        ],
        cost_estimate=small,
        name="plan",
    )(table, near_list)
    zs[0], plan = lax.optimization_barrier((zs[0], plan))

    def across(q, x):
        return lax.ppermute(x, "depth", swaps(sz.n_depth, q))

    numbers, sources = list(range(2 + n_x)), [own, *xs, zs[0]]
    a_shape = ((sz.n_a * BS, 3 * BS), jnp.bfloat16)
    acc_shape = (((sz.n_out + 1) * BS, BS), jnp.float32)
    right, acc = pl.pallas_call(
        functools.partial(early_kernel, sz, numbers),
        out_shape=[
            jax.ShapeDtypeStruct((3 * sz.own * BS, BS), jnp.bfloat16),
            jax.ShapeDtypeStruct(*acc_shape),
        ],
        in_specs=[smem] + [vmem] * len(sources),
        out_specs=[vmem] * 2,
        scratch_shapes=[pltpu.VMEM(*a_shape)],
        compiler_params=params,
        cost_estimate=small,
        name="early",
    )(plan, *sources)
    *far, acc = lax.optimization_barrier((*zs[1:], acc))
    numbers, sources = [2 + n_x + m for m in range(len(far))], list(far)
    for q in range(1, sz.n_depth):
        base = 1 + n_x + q * sz.block
        numbers += [base - 1, base] + [base + 1 + m for m in range(len(far))]
        sources += [across(q, x) for x in (near, zs[0], *far)]
    return pl.pallas_call(
        functools.partial(late_kernel, sz, numbers),
        out_shape=jax.ShapeDtypeStruct(matrix.shape, matrix.dtype),
        in_specs=[smem, anywhere] + [vmem] * (2 + len(sources)),
        out_specs=anywhere,
        input_output_aliases={1: 0},
        scratch_shapes=[pltpu.VMEM(*a_shape), pltpu.VMEM(*acc_shape), pltpu.SemaphoreType.DMA],
        compiler_params=params,
        cost_estimate=small,
        name="late",
    )(plan, zeros, right, acc, *sources)


def shards(sz, matrix, occupancy, pattern):
    smem = pl.BlockSpec(memory_space=pltpu.SMEM)
    vmem = pl.BlockSpec(memory_space=pltpu.VMEM)
    table, near_list, bucket = pl.pallas_call(
        functools.partial(table_kernel, sz),
        out_shape=[
            jax.ShapeDtypeStruct((sz.tables, sz.nb, sz.nb), jnp.int32),
            jax.ShapeDtypeStruct((1, sz.nb), jnp.int32),
            jax.ShapeDtypeStruct((1,), jnp.int32),
        ],
        in_specs=[vmem, vmem],
        out_specs=[vmem, vmem, smem],
        name="tables",
    )(occupancy, pattern)
    branches = [functools.partial(exchange_and_multiply, sz, lengths) for lengths in sz.lengths]
    return lax.switch(bucket[0], branches, matrix, table, near_list)


def solution(mesh):
    def whole(matrix, occupancy, pattern):
        sz = Sizes(mesh, matrix.shape)
        return jax.shard_map(
            functools.partial(shards, sz),
            mesh=mesh,
            in_specs=(P("row", ("col", "depth")), P(), P()),
            out_specs=P("row", ("col", "depth")),
            check_vma=False,
        )(matrix, occupancy, pattern)

    return whole
```

time: 714 us -> 63.8 us (0.09)
  waiting for transfers between devices: 492 us -> 23.2 us
  matrix products: 183 us -> 0 us
  Pallas kernels: 0 us -> 25.7 us
  local copies, waits for them, and re-layouts: 16.9 us -> 1.73 us
  between operations: 13.4 us -> 0.84 us
  starting transfers between devices: 0.04 us -> 11.8 us
    all_gather x2 -> x0, waiting for transfers between devices: 491 us -> none  [the longest x1 325 us: shards(): left_panel = lax.all_gather(masked, ('col', 'depth'), axis=1, tiled=True)]
    dot_general x1 -> x0, matrix products: 183 us -> none  [shards(): jnp.dot(left_panel, lax.all_gather(masked, 'row', axis=0, tiled=True), pr...]
    pallas_call x0 -> x5, Pallas kernels: none -> 25.7 us  [the longest x1 8.89 us: exchange_and_multiply(): pl.pallas_call(functools.partial(plan_kernel, sz), out_shape=[jax.ShapeDt...]
    ppermute x0 -> x10, waiting for transfers between devices: none -> 23.2 us  [the longest x3 20.9 us: exchange_and_multiply(): lax.ppermute(x, 'col', swaps(sz.n_col, m + 1))]
    ppermute x0 -> x10, starting transfers between devices: none -> 11.8 us  [the longest x3 5.49 us: exchange_and_multiply(): lax.ppermute(x, 'col', swaps(sz.n_col, m + 1))]
  transfers between devices with their start and end apart: 2 -> 10, of which waited for: 2 -> 4; matrix products, arithmetic and copies ran while one was open for 1% -> 0% of each run, Pallas kernels for 0% -> 20%
where the time goes in v2:
time: 63.8 us; the launch traced here: 63.7 us
  Pallas kernels  25.7 us (40%)
  waiting for transfers between devices  23.2 us (36%)
  starting transfers between devices  11.8 us (18%)
  local copies, waits for them, and re-layouts  1.73 us (3%)
  between operations  0.84 us (1%)
    ppermute x3, waiting for transfers between devices, exchange_and_multiply(): lax.ppermute(x, 'col', swaps(sz.n_col, m + 1))  20.9 us
    pallas_call x1, Pallas kernels, exchange_and_multiply(): pl.pallas_call(functools.partial(plan_kernel, sz), out_shape=[jax.ShapeDt...  8.89 us
    ppermute x3, starting transfers between devices, exchange_and_multiply(): lax.ppermute(x, 'col', swaps(sz.n_col, m + 1))  5.49 us
    pallas_call x1, Pallas kernels, exchange_and_multiply(): pl.pallas_call(functools.partial(pack_kernel, sz), out_shape=shapes, in_s...  5.15 us
    pallas_call x1, Pallas kernels, exchange_and_multiply(): pl.pallas_call(functools.partial(late_kernel, sz, numbers), out_shape=jax...  4.63 us
    pallas_call x1, Pallas kernels, exchange_and_multiply(): pl.pallas_call(functools.partial(early_kernel, sz, numbers), out_shape=[j...  4.14 us
    ppermute x4, starting transfers between devices, across(): return lax.ppermute(x, 'depth', swaps(sz.n_depth, q))  3.39 us
    ppermute x3, starting transfers between devices, exchange_and_multiply(): lax.ppermute(x, 'row', swaps(sz.n_row, m + 1))  2.95 us
  transfers between devices with their start and end apart: 10, of which 4 were waited for; matrix products, arithmetic and copies ran while one was open for 0% of the time, Pallas kernels for 20%

profile of v2, /device:TPU:11, one launch (start us, length us, event | category | flops | bytes accessed | tf_op | source)
XLA Modules:
  0.0 63.7 jit_solution(11322106837358881224)
XLA Ops:
  0.0 2.9 %tables.1 = (s32[2,48,48]{2,1,0:T(8,128)S(1)}, s32[1,48]{1,0:T(1,128)S(1)}, s32[1]{0:T(128)}) custom-call(s32[48,48]{1,0:T(8,128)} %occ_ref.1, s32[48,48]{1,0:T(8,128)} %pat_ref.1), custom_call_target="tpu_custom_call" | custom-call | tf_op jit(solution)/shard_map/tables/pallas_call | solution.py:533
  3.6 59.9 %conditional.1 = (f32[1536,768]{1,0:T(8,128)}) conditional(s32[]{:T(128)} %bitcast, (s32[2,48,48]{2,1,0:T(8,128)S(1)}, s32[1,48]{1,0:T(1,128)S(1)}, f32[1536,768]{1,0:T(8,128)}) %tuple.45, (s32[2,48,48]{2,1,0:T(8,128)S(1)}, s32[1,48]{1,0:T(1,128)S(1)}, f32[1536,768]{1,0:T(8,128)}) %tuple.45, ...), branch_computations={%region_0.0_spmd, %region_1.0_spmd, %region_2.0_spmd, %region_3.0_... | conditional | bytes 129247824 | solution.py:545
  3.6 0.0 copy-start.35
  3.6 0.0 copy-start.43
  3.6 5.1 %pack.10 = (f32[3072,128]{1,0:T(8,128)S(1)}, f32[1544,128]{1,0:T(8,128)}, f32[1032,128]{1,0:T(8,128)S(1)}, f32[904,128]{1,0:T(8,128)}, f32[904,128]{1,0:T(8,128)...) custom-call(s32[2,48,48]{2,1,0:T(8,128)S(1)} %get-tuple-element.102.table_ref, ...), custom_call_target="tpu_custom_call" | custom-call | bytes 1024 | tf_op jit(solution)/shard_map/cond/branch_2_fun/pack/pallas_call | solution.py:464
  8.8 0.2 collective-permute-start.20
  8.9 0.4 collective-permute-start.21
  9.3 1.8 %collective-permute-start.22 = (f32[1160,128]{1,0:T(8,128)}, f32[1160,128]{1,0:T(8,128)S(1)}, u32[]{:S(2)}, u32[]{:S(2)}) collective-permute-start(f32[1160,128]{1,0:T(8,128)} %get-tuple-element.111), channel_id=1, source_target_pairs={{0,16},{8,24},{16,0},{24,8},{1,17},{9,25},{17,1},{25,9},{2,18},{10... | collective-permute-start | bytes 1781768 | tf_op jit(solution)/shard_map/cond/branch_2_fun/ppermute | solution.py:475
  11.1 0.8 %collective-permute-start.23 = (f32[1160,128]{1,0:T(8,128)}, f32[1160,128]{1,0:T(8,128)}, u32[]{:S(2)}, u32[]{:S(2)}) collective-permute-start(f32[1160,128]{1,0:T(8,128)} %get-tuple-element.112), channel_id=1, source_target_pairs={{0,24},{8,16},{16,8},{24,0},{1,25},{9,17},{17,9},{25,1},{2,26},{10... | collective-permute-start | bytes 1781768 | tf_op jit(solution)/shard_map/cond/branch_2_fun/ppermute | solution.py:475
  11.9 2.5 %collective-permute-start.24 = (f32[904,128]{1,0:T(8,128)}, f32[904,128]{1,0:T(8,128)}, u32[]{:S(2)}, u32[]{:S(2)}) collective-permute-start(f32[904,128]{1,0:T(8,128)} %get-tuple-element.115), channel_id=1, source_target_pairs={{0,4},{2,6},{4,0},{6,2},{1,5},{3,7},{5,1},{7,3},{8,12},{10,14},{12... | collective-permute-start | bytes 1388552 | tf_op jit(solution)/shard_map/cond/branch_2_fun/ppermute | solution.py:474
  14.4 12.7 %collective-permute-done.20.rest_4_ = f32[1032,128]{1,0:T(8,128)S(1)} collective-permute-done((f32[1032,128]{1,0:T(8,128)S(1)}, f32[1032,128]{1,0:T(8,128)S(1)}, u32[]{:S(2)}, u32[]{:S(2)}) %collective-permute-start.20) | collective-permute-done | bytes 528416 | tf_op jit(solution)/shard_map/cond/branch_2_fun/ppermute | solution.py:474
  27.2 2.8 %collective-permute-start.25 = (f32[904,128]{1,0:T(8,128)}, f32[904,128]{1,0:T(8,128)}, u32[]{:S(2)}, u32[]{:S(2)}) collective-permute-start(f32[904,128]{1,0:T(8,128)} %get-tuple-element.116), channel_id=1, source_target_pairs={{0,6},{2,4},{4,2},{6,0},{1,7},{3,5},{5,3},{7,1},{8,14},{10,12},{12... | collective-permute-start | bytes 1388552 | tf_op jit(solution)/shard_map/cond/branch_2_fun/ppermute | solution.py:474
  30.0 0.0 collective-permute-done.21.rest_1_
  30.0 0.0 copy-done.11
  30.0 1.3 %collective-permute-start.26 = (f32[1544,128]{1,0:T(8,128)}, f32[1544,128]{1,0:T(8,128)S(1)}, u32[]{:S(2)}, u32[]{:S(2)}) collective-permute-start(f32[1544,128]{1,0:T(8,128)} %get-tuple-element.121), channel_id=1, source_target_pairs={{0,1},{1,0},{2,3},{3,2},{4,5},{5,4},{6,7},{7,6},{8,9},{9,8},{10,11... | collective-permute-start | bytes 2371592 | tf_op jit(solution)/shard_map/cond/branch_2_fun/ppermute | solution.py:493
  31.3 8.9 %plan.10 = (s32[421]{0:T(512)}, f32[1536,768]{1,0:T(8,128)}) custom-call(s32[2,48,48]{2,1,0:T(8,128)} %copy-done.35, s32[1,48]{1,0:T(1,128)} %copy-done.43), custom_call_target="tpu_custom_call" | custom-call | bytes 1024 | tf_op jit(solution)/shard_map/cond/branch_2_fun/plan/pallas_call | solution.py:476
  40.2 0.0 collective-permute-done.22.rest_2_
  40.2 0.1 collective-permute-start.27
  40.3 0.0 collective-permute-done.23.rest_3_
  40.3 0.0 copy-start.12
  40.3 1.0 %copy-done.12 = f32[1032,128]{1,0:T(8,128)S(1)} copy-done((f32[1032,128]{1,0:T(8,128)S(1)}, f32[1032,128]{1,0:T(8,128)}, u32[]{:S(2)}) %copy-start.12) | copy-done | bytes 528408 | tf_op jit(solution)/shard_map/cond
  41.3 0.7 %copy-done.15 = s32[421]{0:T(512)S(1)} copy-done((s32[421]{0:T(512)S(1)}, s32[421]{0:T(512)}, u32[]{:S(2)}) %copy-start.15) | copy-done | bytes 1708 | tf_op jit(solution)/shard_map/cond
  42.0 4.1 %early.10 = (bf16[9216,128]{1,0:T(8,128)(2,1)S(1)}, f32[9344,128]{1,0:T(8,128)S(1)}) custom-call(s32[421]{0:T(512)S(1)} %copy-done.15, f32[3072,128]{1,0:T(8,128)S(1)} %get-tuple-element.109.rest_0_, f32[1160,128]{1,0:T(8,128)S(1)} %collective-permute-done.21.rest_1_, f32[1160,128]{1,0:T(8,128)S(1)} %collective-permute-done.22.rest_2_, ...), custom_call_target="tpu_custom_call" | custom-call | bytes 1024 | tf_op jit(solution)/shard_map/cond/branch_2_fun/early/pallas_call | solution.py:498
  46.2 0.0 collective-permute-done.24.rest_0_
  46.2 8.1 %collective-permute-done.25.rest_1_ = f32[904,128]{1,0:T(8,128)} collective-permute-done((f32[904,128]{1,0:T(8,128)}, f32[904,128]{1,0:T(8,128)}, u32[]{:S(2)}, u32[]{:S(2)}) %collective-permute-start.25) | collective-permute-done | bytes 462880 | tf_op jit(solution)/shard_map/cond/branch_2_fun/ppermute | solution.py:474
  54.3 2.0 %collective-permute-start.28 = (f32[904,128]{1,0:T(8,128)}, f32[904,128]{1,0:T(8,128)S(1)}, u32[]{:S(2)}, u32[]{:S(2)}) collective-permute-start(f32[904,128]{1,0:T(8,128)} %collective-permute-done.24.rest_0_), channel_id=1, source_target_pairs={{0,1},{1,0},{2,3},{3,2},{4,5},{5,4},{6,7},{7,6},{8,9},{9,8},{10,11... | collective-permute-start | bytes 1388552 | tf_op jit(solution)/shard_map/cond/branch_2_fun/ppermute | solution.py:493
  56.3 0.0 collective-permute-start.29
  56.3 0.0 collective-permute-done.26.rest_2_
  56.3 1.7 %collective-permute-done.28.rest_4_ = f32[904,128]{1,0:T(8,128)S(1)} collective-permute-done((f32[904,128]{1,0:T(8,128)}, f32[904,128]{1,0:T(8,128)S(1)}, u32[]{:S(2)}, u32[]{:S(2)}) %collective-permute-start.28) | collective-permute-done | bytes 462880 | tf_op jit(solution)/shard_map/cond/branch_2_fun/ppermute | solution.py:493
  58.0 0.7 %collective-permute-done.29.rest_5_ = f32[904,128]{1,0:T(8,128)S(1)} collective-permute-done((f32[904,128]{1,0:T(8,128)}, f32[904,128]{1,0:T(8,128)S(1)}, u32[]{:S(2)}, u32[]{:S(2)}) %collective-permute-start.29) | collective-permute-done | bytes 462880 | tf_op jit(solution)/shard_map/cond/branch_2_fun/ppermute | solution.py:493
  58.6 0.0 collective-permute-done.27.rest_3_
  58.6 4.6 %late.10 = f32[1536,768]{1,0:T(8,128)} custom-call(s32[421]{0:T(512)S(1)} %copy-done.16, f32[1536,768]{1,0:T(8,128)} %get-tuple-element.108.zeros_ref, bf16[9216,128]{1,0:T(8,128)(2,1)S(1)} %get-tuple-element.114.b_ref, f32[9344,128]{1,0:T(8,128)S(1)} %get-tuple-element.118.before_ref, ...), custom_call_target="tpu_custom_call", output_to_operand_aliasing={{}: (1, {})} | custom-call | bytes 1024 | tf_op jit(solution)/shard_map/cond/branch_2_fun/late/pallas_call | solution.py:517
  (6 shorter events, 0.0 us)
Async XLA Ops:
  3.6 5.2 %copy-start.35 = (s32[2,48,48]{2,1,0:T(8,128)}, s32[2,48,48]{2,1,0:T(8,128)S(1)}, u32[]{:S(2)}) copy-start(s32[2,48,48]{2,1,0:T(8,128)S(1)} %get-tuple-element.102.table_ref) | copy-start | bytes 55300 | tf_op jit(solution)/shard_map/cond
  3.6 5.2 %copy-start.43 = (s32[1,48]{1,0:T(1,128)}, s32[1,48]{1,0:T(1,128)S(1)}, u32[]{:S(2)}) copy-start(s32[1,48]{1,0:T(1,128)S(1)} %get-tuple-element.103.near_ref) | copy-start | bytes 580 | tf_op jit(solution)/shard_map/cond
  8.8 18.4 %collective-permute-start.20 = (f32[1032,128]{1,0:T(8,128)S(1)}, f32[1032,128]{1,0:T(8,128)S(1)}, u32[]{:S(2)}, u32[]{:S(2)}) collective-permute-start(f32[1032,128]{1,0:T(8,128)S(1)} %get-tuple-element.105), channel_id=1, source_target_pairs={{0,2},{2,0},{4,6},{6,4},{1,3},{3,1},{5,7},{7,5},{8,10},{10,8},{12,... | collective-permute-start | bytes 1585160 | tf_op jit(solution)/shard_map/cond/branch_2_fun/ppermute | solution.py:474
  8.9 21.0 %collective-permute-start.21 = (f32[1160,128]{1,0:T(8,128)S(1)}, f32[1160,128]{1,0:T(8,128)S(1)}, u32[]{:S(2)}, u32[]{:S(2)}) collective-permute-start(f32[1160,128]{1,0:T(8,128)S(1)} %get-tuple-element.110), channel_id=1, source_target_pairs={{0,8},{8,0},{16,24},{24,16},{1,9},{9,1},{17,25},{25,17},{2,10},{10... | collective-permute-start | bytes 1781768 | tf_op jit(solution)/shard_map/cond/branch_2_fun/ppermute | solution.py:475
  9.3 30.9 %collective-permute-start.22 = (f32[1160,128]{1,0:T(8,128)}, f32[1160,128]{1,0:T(8,128)S(1)}, u32[]{:S(2)}, u32[]{:S(2)}) collective-permute-start(f32[1160,128]{1,0:T(8,128)} %get-tuple-element.111), channel_id=1, source_target_pairs={{0,16},{8,24},{16,0},{24,8},{1,17},{9,25},{17,1},{25,9},{2,18},{10... | collective-permute-start | bytes 1781768 | tf_op jit(solution)/shard_map/cond/branch_2_fun/ppermute | solution.py:475
  11.1 29.2 %collective-permute-start.23 = (f32[1160,128]{1,0:T(8,128)}, f32[1160,128]{1,0:T(8,128)}, u32[]{:S(2)}, u32[]{:S(2)}) collective-permute-start(f32[1160,128]{1,0:T(8,128)} %get-tuple-element.112), channel_id=1, source_target_pairs={{0,24},{8,16},{16,8},{24,0},{1,25},{9,17},{17,9},{25,1},{2,26},{10... | collective-permute-start | bytes 1781768 | tf_op jit(solution)/shard_map/cond/branch_2_fun/ppermute | solution.py:475
  11.9 34.3 %collective-permute-start.24 = (f32[904,128]{1,0:T(8,128)}, f32[904,128]{1,0:T(8,128)}, u32[]{:S(2)}, u32[]{:S(2)}) collective-permute-start(f32[904,128]{1,0:T(8,128)} %get-tuple-element.115), channel_id=1, source_target_pairs={{0,4},{2,6},{4,0},{6,2},{1,5},{3,7},{5,1},{7,3},{8,12},{10,14},{12... | collective-permute-start | bytes 1388552 | tf_op jit(solution)/shard_map/cond/branch_2_fun/ppermute | solution.py:474
  27.2 2.8 %copy-start.11 = (f32[1032,128]{1,0:T(8,128)}, f32[1032,128]{1,0:T(8,128)S(1)}, u32[]{:S(2)}) copy-start(f32[1032,128]{1,0:T(8,128)S(1)} %collective-permute-done.20.rest_4_) | copy-start | bytes 1585156 | tf_op jit(solution)/shard_map/cond
  27.2 27.1 %collective-permute-start.25 = (f32[904,128]{1,0:T(8,128)}, f32[904,128]{1,0:T(8,128)}, u32[]{:S(2)}, u32[]{:S(2)}) collective-permute-start(f32[904,128]{1,0:T(8,128)} %get-tuple-element.116), channel_id=1, source_target_pairs={{0,6},{2,4},{4,2},{6,0},{1,7},{3,5},{5,3},{7,1},{8,14},{10,12},{12... | collective-permute-start | bytes 1388552 | tf_op jit(solution)/shard_map/cond/branch_2_fun/ppermute | solution.py:474
  30.0 26.3 %collective-permute-start.26 = (f32[1544,128]{1,0:T(8,128)}, f32[1544,128]{1,0:T(8,128)S(1)}, u32[]{:S(2)}, u32[]{:S(2)}) collective-permute-start(f32[1544,128]{1,0:T(8,128)} %get-tuple-element.121), channel_id=1, source_target_pairs={{0,1},{1,0},{2,3},{3,2},{4,5},{5,4},{6,7},{7,6},{8,9},{9,8},{10,11... | collective-permute-start | bytes 2371592 | tf_op jit(solution)/shard_map/cond/branch_2_fun/ppermute | solution.py:493
  40.2 18.5 %copy-start.16 = (s32[421]{0:T(512)S(1)}, s32[421]{0:T(512)}, u32[]{:S(2)}) copy-start(s32[421]{0:T(512)} %get-tuple-element.107.plan_ref) | copy-start | bytes 5056 | tf_op jit(solution)/shard_map/cond
  40.2 18.4 %collective-permute-start.27 = (f32[1032,128]{1,0:T(8,128)}, f32[1032,128]{1,0:T(8,128)S(1)}, u32[]{:S(2)}, u32[]{:S(2)}) collective-permute-start(f32[1032,128]{1,0:T(8,128)} %copy-done.11), channel_id=1, source_target_pairs={{0,1},{1,0},{2,3},{3,2},{4,5},{5,4},{6,7},{7,6},{8,9},{9,8},{10,11... | collective-permute-start | bytes 1585160 | tf_op jit(solution)/shard_map/cond/branch_2_fun/ppermute | solution.py:493
  40.3 1.0 %copy-start.12 = (f32[1032,128]{1,0:T(8,128)S(1)}, f32[1032,128]{1,0:T(8,128)}, u32[]{:S(2)}) copy-start(f32[1032,128]{1,0:T(8,128)} %copy-done.11) | copy-start | bytes 1585156 | tf_op jit(solution)/shard_map/cond
  41.3 0.7 %copy-start.15 = (s32[421]{0:T(512)S(1)}, s32[421]{0:T(512)}, u32[]{:S(2)}) copy-start(s32[421]{0:T(512)} %get-tuple-element.107.plan_ref) | copy-start | bytes 5056 | tf_op jit(solution)/shard_map/cond
  54.3 3.7 %collective-permute-start.28 = (f32[904,128]{1,0:T(8,128)}, f32[904,128]{1,0:T(8,128)S(1)}, u32[]{:S(2)}, u32[]{:S(2)}) collective-permute-start(f32[904,128]{1,0:T(8,128)} %collective-permute-done.24.rest_0_), channel_id=1, source_target_pairs={{0,1},{1,0},{2,3},{3,2},{4,5},{5,4},{6,7},{7,6},{8,9},{9,8},{10,11... | collective-permute-start | bytes 1388552 | tf_op jit(solution)/shard_map/cond/branch_2_fun/ppermute | solution.py:493
  56.3 2.3 %collective-permute-start.29 = (f32[904,128]{1,0:T(8,128)}, f32[904,128]{1,0:T(8,128)S(1)}, u32[]{:S(2)}, u32[]{:S(2)}) collective-permute-start(f32[904,128]{1,0:T(8,128)} %collective-permute-done.25.rest_1_), channel_id=1, source_target_pairs={{0,1},{1,0},{2,3},{3,2},{4,5},{5,4},{6,7},{7,6},{8,9},{9,8},{10,11... | collective-permute-start | bytes 1388552 | tf_op jit(solution)/shard_map/cond/branch_2_fun/ppermute | solution.py:493
